TPU v7x, 256 devices: a whole 4x4x8 slice. The times are simulated.
256 devices in a mesh: diag: 256 (over x, y, z, core).
Axes of the slice: x: 4, y: 4, z: 8, core: 2. Of those that a mesh axis runs over, the one named last changes fastest.
Arguments:
- features: bfloat16 [8192, 256], P('diag'), may hold values from -6 to 6
- row_proj: bfloat16 [256, 32], replicated, may hold values from -0.375 to 0.375
- col_proj: bfloat16 [256, 32], replicated, may hold values from -0.375 to 0.375
- first_filter: bfloat16 [3, 3, 32, 32], replicated, may hold values from -0.375 to 0.375
- second_filter: bfloat16 [3, 3, 32, 32], replicated, may hold values from -0.375 to 0.375
- readout: bfloat16 [32], replicated, may hold values from -1 to 1
- target: float32 [8192, 256], P('diag'), may hold values from -6 to 6
Outputs:
- grad_features: float32 [8192, 256], P('diag')
- grad_row_proj: float32 [256, 32], replicated
- grad_col_proj: float32 [256, 32], replicated
- grad_conv_one: float32 [3, 3, 32, 32], replicated
- grad_conv_two: float32 [3, 3, 32, 32], replicated
- grad_readout: float32 [32], replicated
All inputs are finite; a program needn't handle non-finite values.
Results may differ from a plain program's by a relative error of at most 0.0006.
Values may be sent and summed in bfloat16 or wider, within the bound.
A program may use at most 128 MiB of HBM per device.

v0:
```python
import functools
import math

import jax
import jax.numpy as jnp
from jax import lax
from jax.experimental import pallas as pl
from jax.experimental.pallas import tpu as pltpu
from jax.sharding import PartitionSpec as P

MESH = pl.DeviceIdType.MESH
F32, BF16 = jnp.float32, jnp.bfloat16

ROWS = 32
BAND = 256
PAIR = 32
HALO = 12
GROUPS = (ROWS + 2 * HALO) // 4
FIRST_OWN, LAST_OWN = 3, 10
PAD = 16
LENGTH = 352
WIDE, SPAN, CHUNK = 272, 264, 88
AHEAD = 9
REACH = 8
C0 = math.sqrt(2.0 / math.pi)
C1 = C0 * 0.044715
SIDE = 16
TOTAL = 256
SEM = pltpu.SemaphoreType.DMA


def iota(shape, dim):
    return lax.broadcasted_iota(jnp.int32, shape, dim)


def lane_block(rows):
    return lax.shift_right_logical(iota((rows, 128), 1), 5)


def gelu(x, with_slope):
    cubic = C1 * (x * x)
    s = 0.5 * jnp.tanh(x * (cubic + C0)) + 0.5
    value = x * s
    slope = s + value * (1.0 - s) * (6.0 * cubic + 2.0 * C0) if with_slope else None
    return value.astype(BF16).astype(F32), slope


def split(x):
    high = x.astype(BF16)
    return high, (x - high.astype(F32)).astype(BF16)


def fold(x):
    total = x[0:8]
    for i in range(1, x.shape[0] // 8):
        total = total + x[8 * i : 8 * i + 8]
    return total


def dot(a, b):
    return jnp.dot(a, b, preferred_element_type=F32)


def dot_t(a, b):
    return lax.dot_general(a, b, (((0,), (0,)), ((), ())), preferred_element_type=F32)


def dot_nt(a, b):
    return lax.dot_general(a, b, (((1,), (1,)), ((), ())), preferred_element_type=F32)


def repeater(lanes):
    return (jnp.bitwise_and(iota((PAIR, lanes), 1), 31) == iota((PAIR, lanes), 0)).astype(F32).astype(BF16)


def spread(block):
    turned = [block] + [pltpu.roll(block, 32 * s, 1) for s in (1, 2, 3)]
    where_block = lane_block(8)
    outs = []
    for b in range(4):
        value = turned[(3 - b) % 4]
        for other in range(3):
            value = jnp.where(where_block == other, turned[(other - b) % 4], value)
        outs.append(value)
    return outs


def step_kernel(
    n, feat_in, row_in, col_in, target_in, k1_in, k2_in, ro, red,
    feat, row_t, col_t, target, k1, k2,
    proj, sbuf, rbuf, tlow, thigh, roww, w1, wa, w2, rol, colr, mk, ts, act0, d0, act1, f1, d1, mis, g1,
    lhs, lhs2, k2t, res, qbuf, wq, xall, gall, fg, tacc, colacc, tiles, colp, rowg, cbuf, vbuf, arbuf, rsbuf, bbuf, mine, gbuf,
    loads, sems,
):
    me = lax.axis_index("diag")
    start = me * ROWS
    side = n // SIDE
    part = TOTAL // side
    pos = lax.rem(me, SIDE)
    plane = lax.div(me, SIDE)

    def dev(step):
        return lax.rem(me + step + n, n)

    def in_line(s):
        return me - pos + lax.rem(pos + s, SIDE)

    def across(s):
        return lax.rem(plane + s, side) * SIDE + pos

    fetches = [
        pltpu.make_async_copy(source, place, loads.at[i])
        for i, (source, place) in enumerate(
            ((feat_in, feat), (row_in, row_t), (col_in, col_t), (k1_in, k1), (k2_in, k2), (target_in, target))
        )
    ]
    for fetch in fetches:
        fetch.start()

    barrier = pltpu.get_barrier_semaphore()
    for step in range(1, AHEAD + 1):
        for target_device in (dev(step), dev(-step)):
            pl.semaphore_signal(barrier, inc=1, device_id=(target_device,), device_id_type=MESH)

    def greet(sign, s, carry):
        pl.semaphore_signal(barrier, inc=1, device_id=(me + sign * s,), device_id_type=MESH)
        return carry

    lax.fori_loop(AHEAD + 1, SIDE - pos, functools.partial(greet, 1), 0)
    lax.fori_loop(AHEAD + 1, pos + 1, functools.partial(greet, -1), 0)

    def greet_across(s, carry):
        pl.semaphore_signal(barrier, inc=1, device_id=(across(s),), device_id_type=MESH)
        return carry

    lax.fori_loop(1, side, greet_across, 0)

    for fetch in fetches[0:3]:
        fetch.wait()
    proj[...] = dot_nt(feat[...], jnp.concatenate([row_t[...]] * 4, axis=0))
    cc = dot_nt(feat[...], jnp.concatenate([col_t[...]] * 4, axis=0))
    where_block = lane_block(8)
    row_c = jnp.zeros((8, 128), F32)
    col_c = jnp.zeros((8, 128), F32)
    for b in range(4):
        row_c = jnp.where(where_block == b, proj[pl.ds(b, 8, stride=4), :], row_c)
        col_c = jnp.where(where_block == b, cc[8 * b : 8 * b + 8], col_c)
    sbuf[0:8] = col_c
    sbuf[8:16] = row_c
    greeted = jnp.maximum(SIDE - AHEAD - 1 - pos, 0) + jnp.maximum(pos - AHEAD, 0)
    pl.semaphore_wait(barrier, 2 * AHEAD + greeted + side - 1)
    gathers = []
    for slot, step in ((0, 1), (2, -1)):
        gathers.append(
            pltpu.make_async_remote_copy(sbuf, rbuf.at[slot], sems.at[0], sems.at[1], device_id=(dev(step),), device_id_type=MESH)
        )
    for m in range(3, AHEAD + 2):
        gathers.append(
            pltpu.make_async_remote_copy(
                sbuf.at[pl.ds(0, 8)], rbuf.at[m, pl.ds(0, 8)], sems.at[0], sems.at[1], device_id=(dev(1 - m),), device_id_type=MESH
            )
        )
    gathers.append(
        pltpu.make_async_remote_copy(
            target_in.at[pl.ds(24, 8)], tlow, sems.at[0], sems.at[1], device_id=(dev(1),), device_id_type=MESH
        )
    )
    gathers.append(
        pltpu.make_async_remote_copy(
            target_in.at[pl.ds(0, 8)], thigh, sems.at[0], sems.at[1], device_id=(dev(-1),), device_id_type=MESH
        )
    )
    for copy in gathers:
        copy.start()

    for fetch in fetches[3:6]:
        fetch.wait()
    rep8 = repeater(256)
    where_out = lax.shift_right_logical(iota((PAIR, 256), 1), 5)

    def build(weights, sign):
        for q in range(3):
            for place, ri in enumerate((8, 9, -2, -1, 0, 1, 2, 3, 4, 5, 6, 7)):
                value = jnp.zeros((PAIR, 256), F32)
                for p in range(3):
                    tap = 3 * p + q
                    ro_here = ri - sign * 2 * (p - 1)
                    if 0 <= ro_here < 8:
                        value = jnp.where(where_out == ro_here, tiles[32 * tap : 32 * tap + 32], value)
                row = (q * 12 + place) * 32
                weights[row : row + 32] = value.astype(BF16)

    tiles[...] = dot(k1[...], rep8)
    build(w1, 1)
    for tap in range(9):
        tiles[32 * tap : 32 * tap + 32] = dot_t(k1[32 * tap : 32 * tap + 32], rep8)
    build(wa, -1)
    ro8 = jnp.broadcast_to(ro[...].astype(F32), (8, PAIR)).astype(BF16)
    rol[...] = dot(ro8, repeater(128))
    for tap in range(9):
        for b in range(4):
            row = 128 * tap + 32 * b
            k2t[row : row + 32] = k2[32 * tap : 32 * tap + 32]
        w2[8 * tap : 8 * tap + 8] = dot_nt(ro8, k2t[128 * tap : 128 * tap + 128])
    gbuf[320:328] = rol[...]

    same = lax.shift_right_logical(iota((256, 256), 0), 5) == lax.shift_right_logical(iota((256, 256), 1), 5)
    ones = same.astype(F32).astype(BF16)
    wq[0:256] = ones
    wq[256:512] = ones
    act0[0] = jnp.zeros((LENGTH, 128), F32)
    act0[GROUPS + 1] = jnp.zeros((LENGTH, 128), F32)
    colacc[...] = jnp.zeros((LENGTH, 128), F32)
    tacc[...] = jnp.zeros((80, 128), F32)
    ts[...] = jnp.zeros((LENGTH, 128), F32)
    arbuf[224:256] = jnp.zeros((32, 128), F32)
    column = iota((LENGTH, 128), 0) - PAD
    mk[...] = jnp.where(column + (start - HALO) < n * ROWS, column - lane_block(LENGTH), 1 << 20)

    def all_of(place, sem):
        pltpu.make_async_copy(place, place, sem).wait()

    all_of(arbuf.at[pl.ds(0, 128)], sems.at[1])
    for m in range(AHEAD + 2):
        for b, value in enumerate(spread(col_c if m == 1 else rbuf[m, 0:8])):
            row = 32 * (m - 1) + 8 * b + HALO + PAD
            if row >= 0 and row + 8 <= LENGTH:
                colr[row : row + 8] = value
    roww[0:8] = rbuf[0, 8:16]
    roww[8:16] = row_c
    roww[16:24] = rbuf[2, 8:16]
    wide = jnp.concatenate([tlow[...], target[...], thigh[...]], axis=0)
    wide = jnp.concatenate([wide, jnp.zeros((48, 128), F32)], axis=1)
    wide = jnp.concatenate([wide, jnp.zeros((80, 384), F32)], axis=0)
    sheared = pltpu.roll(wide, 0, 1, stride=1, stride_axis=0)
    ts[4 + PAD : 4 + PAD + 312] = sheared.T[0:312]

    def first_column(u):
        return pl.multiple_of(8 * lax.shift_right_logical(u, 1), 8)

    def mask_at(u, row, count):
        shift = 4 * u - jnp.where(start + 4 * u - HALO >= 0, 0, 1 << 20)
        return jnp.bitwise_and(mk[pl.ds(row, count), :] - shift, -BAND) == 0

    def clear_sides(buffer, index, base):
        buffer[index, pl.ds(base, 16), :] = jnp.zeros((16, 128), F32)
        buffer[index, pl.ds(base + PAD + SPAN, 24), :] = jnp.zeros((24, 128), F32)

    left = lane_block(WIDE) < 2

    def pieces(buffer, index, row):
        ends = jnp.where(left, buffer[index + 3, pl.ds(row, WIDE), :], buffer[index, pl.ds(row, WIDE), :])
        return ends, buffer[index + 1, pl.ds(row, WIDE), :], buffer[index + 2, pl.ds(row, WIDE), :]

    def make_field(with_slope, v):
        base = pl.multiple_of(8 * v, 8)
        for h in range(2):
            u = 2 * v + h
            clear_sides(act0, u + 1, base)
            row_here = roww[pl.ds(u + 5, 1), :]
            for ch in range(3):
                row = base + PAD + CHUNK * ch
                mask = mask_at(u, row, CHUNK)
                x = jnp.where(mask, row_here + colr[pl.ds(row, CHUNK), :], 0.0)
                act, slope = gelu(x, with_slope)
                act0[u + 1, pl.ds(row, CHUNK), :] = act
                if with_slope:
                    d0[u, pl.ds(row, CHUNK), :] = jnp.where(mask, slope, 0.0)

    def conv_operand(v):
        base = pl.multiple_of(8 * v, 8)
        for q in range(3):
            for d, piece in enumerate(pieces(act0, 2 * v, base + PAD + 2 * (q - 1))):
                lhs[:, 128 * (3 * q + d) : 128 * (3 * q + d + 1)] = piece.astype(BF16)

    def conv():
        res[0:WIDE] = dot(lhs[...], w1[...])

    def conv_result(with_slope, v):
        base = pl.multiple_of(8 * v, 8)
        for h in range(2):
            u = 2 * v + h
            clear_sides(act1, u, base)
            clear_sides(f1, u, base)
            row_here = roww[pl.ds(u + 5, 1), :]
            for ch in range(3):
                row = base + PAD + CHUNK * ch
                added = res[CHUNK * ch : CHUNK * ch + CHUNK, 128 * h : 128 * h + 128]
                mask = mask_at(u, row, CHUNK)
                x = jnp.where(mask, (row_here + colr[pl.ds(row, CHUNK), :]) + added, 0.0)
                act, slope = gelu(x, with_slope)
                act1[u, pl.ds(row, CHUNK), :] = act
                f1[u, pl.ds(row, CHUNK), :] = x
                if with_slope:
                    d1[u, pl.ds(row, CHUNK), :] = jnp.where(mask, slope, 0.0)

    make_field(False, 0)
    make_field(True, 1)
    conv_operand(0)
    make_field(True, 2)
    conv()

    def first_conv(with_field, v, carry):
        conv_operand(v)
        conv_result(True, v - 1)
        if with_field:
            make_field(True, v + 2)
        conv()
        return carry

    lax.fori_loop(1, 5, functools.partial(first_conv, True), 0)
    lax.fori_loop(5, 7, functools.partial(first_conv, False), 0)
    conv_result(False, 6)

    def make_misfit(w, carry):
        base = pl.multiple_of(8 * w, 8)
        for at, count in ((0, 96), (96, 96), (192, 80)):
            row = base + PAD + at
            for h in range(2):
                u = 2 * w + 1 + h
                value = rol[0:1] * f1[u, pl.ds(row, count), :]
                for p in range(3):
                    for q in range(3):
                        tap = 3 * p + q
                        value = value + w2[8 * tap : 8 * tap + 1] * act1[u + p - 1, pl.ds(row + 4 * (q - 1), count), :]
                high, low = split(value)
                qbuf[at : at + count, 128 * h : 128 * h + 128] = high
                qbuf[at : at + count, 256 + 128 * h : 384 + 128 * h] = low
            high, low = split(ts[pl.ds(row, count), :])
            qbuf[at : at + count, 512:640] = high
            qbuf[at : at + count, 640:768] = low
        pick = jnp.where(iota((128, 256), 0) == 8 * w + lax.shift_right_logical(iota((128, 256), 1), 5), -1.0, 0.0).astype(BF16)
        wq[512:640] = pick
        wq[640:768] = pick
        value = dot(qbuf[...], wq[...]) * (1.0 / BAND)
        for h in range(2):
            u = 2 * w + 1 + h
            clear_sides(mis, u, base)
            for at, count in ((0, 96), (96, 96), (192, 80)):
                row = base + PAD + at
                mis[u, pl.ds(row, count), :] = jnp.where(
                    mask_at(u, row, count), value[at : at + count, 128 * h : 128 * h + 128], 0.0
                )
        return carry

    lax.fori_loop(0, 6, make_misfit, 0)

    def make_cotangent(u, carry):
        base = first_column(u)
        clear_sides(g1, u, base)
        sums = [None] * 10
        for ch in range(3):
            row = base + PAD + CHUNK * ch
            act = act1[u, pl.ds(row, CHUNK), :]
            back = None
            for p in range(3):
                for q in range(3):
                    tap = 3 * p + q
                    m = mis[u - (p - 1), pl.ds(row - 4 * (q - 1), CHUNK), :]
                    term = w2[8 * tap : 8 * tap + 1] * m
                    back = term if back is None else back + term
                    part = fold(act * m)
                    sums[tap] = part if sums[tap] is None else sums[tap] + part
            m = mis[u, pl.ds(row, CHUNK), :]
            part = fold(m * f1[u, pl.ds(row, CHUNK), :])
            sums[9] = part if sums[9] is None else sums[9] + part
            g1[u, pl.ds(row, CHUNK), :] = rol[0:1] * m + d1[u, pl.ds(row, CHUNK), :] * back
        for tap in range(10):
            source = u - (tap // 3 - 1) if tap < 9 else u
            own = jnp.logical_and(source >= FIRST_OWN, source <= LAST_OWN)
            tacc[8 * tap : 8 * tap + 8] += jnp.where(own, sums[tap], 0.0)
        return carry

    lax.fori_loop(2, GROUPS - 2, make_cotangent, 0)

    def adjoint_operand(w):
        base = pl.multiple_of(8 * w + 8, 8)
        for q in range(3):
            for d, piece in enumerate(pieces(g1, 2 * w + 2, base + PAD - 2 * (q - 1))):
                high, low = split(piece)
                lanes = slice(128 * (3 * q + d), 128 * (3 * q + d + 1))
                lhs2[0:WIDE, lanes] = high
                lhs2[WIDE : 2 * WIDE, lanes] = low

    def adjoint():
        res[...] = dot(lhs2[...], wa[...])

    def adjoint_result(w):
        base = pl.multiple_of(8 * w + 8, 8)
        for h in range(2):
            u = 2 * w + 3 + h
            total_row = None
            for ch in range(3):
                at = CHUNK * ch + 8 * h
                row = base + PAD + at
                lanes = slice(128 * h, 128 * h + 128)
                back = res[at : at + CHUNK, lanes] + res[WIDE + at : WIDE + at + CHUNK, lanes]
                value = g1[u, pl.ds(row, CHUNK), :] + d0[u, pl.ds(row, CHUNK), :] * back
                colacc[pl.ds(row, CHUNK), :] += value
                part = fold(value)
                total_row = part if total_row is None else total_row + part
            rowg[pl.ds(u - 3, 1), :] = jnp.sum(total_row, axis=0, keepdims=True)

    def collect(w):
        for h in range(2):
            u = 2 * w + 3 + h
            base = pl.multiple_of(8 * w + 8 + 8 * h, 8)
            at = pl.multiple_of(WIDE * (2 * w + h), 16)
            high, low = split(g1[u, pl.ds(base + PAD, WIDE), :])
            gall[pl.ds(at, WIDE), 0:128] = high
            gall[pl.ds(at, WIDE), 128:256] = low
            for q in range(3):
                row = base + PAD + 2 * (q - 1)
                ends = jnp.where(left, act0[u + 2, pl.ds(row, WIDE), :], act0[u, pl.ds(row, WIDE), :])
                xall[pl.ds(at, WIDE), 256 * q : 256 * q + 128] = ends.astype(BF16)
                xall[pl.ds(at, WIDE), 256 * q + 128 : 256 * q + 256] = act0[u + 1, pl.ds(row, WIDE), :].astype(BF16)

    adjoint_operand(0)
    collect(0)
    adjoint()

    def first_adjoint(w, carry):
        adjoint_operand(w)
        adjoint_result(w - 1)
        collect(w)
        adjoint()
        return carry

    lax.fori_loop(1, 4, first_adjoint, 0)
    adjoint_result(3)

    where_block = lane_block(8)
    for m in range(REACH + 1):
        packed = jnp.zeros((8, 128), F32)
        for b in range(4):
            row = 32 * m + 8 * b + HALO + PAD
            value = colacc[row : row + 8]
            value = value + pltpu.roll(value, 64, 1)
            value = value + pltpu.roll(value, 32, 1)
            packed = jnp.where(where_block == b, value, packed)
        colp[8 * m : 8 * m + 8] = packed
    columns = []
    for m in range(1, REACH + 1):
        columns.append(
            pltpu.make_async_remote_copy(
                colp.at[pl.ds(8 * m, 8)], cbuf.at[m - 1], sems.at[2], sems.at[3], device_id=(dev(m),), device_id_type=MESH
            )
        )
    for copy in columns:
        copy.start()

    fg[...] = dot_t(gall[...], xall[...])

    where_block = lane_block(32)
    for group in range(3):
        packed = jnp.zeros((32, 128), F32)
        for place in range(4):
            tap = 4 * group + place
            if tap > 8:
                continue
            p, q = tap // 3 - 1, tap % 3
            value = jnp.zeros((32, 128), F32)
            for b in range(4):
                source = b + 2 * p
                lanes = 256 * q + (128 if 0 <= source < 4 else 0)
                both = fg[32 * b : 32 * b + 32, lanes : lanes + 128] + fg[128 + 32 * b : 160 + 32 * b, lanes : lanes + 128]
                value = value + jnp.where(where_block == source % 4, both, 0.0)
            value = value + pltpu.roll(value, 64, 1)
            value = value + pltpu.roll(value, 32, 1)
            packed = jnp.where(where_block == place, value, packed)
        arbuf[128 + 32 * group : 160 + 32 * group] = packed
    for tap in range(10):
        arbuf[224 + tap : 225 + tap] = jnp.sum(tacc[8 * tap : 8 * tap + 8], axis=0, keepdims=True)
    sums = arbuf[224:240]
    sums = sums + pltpu.roll(sums, 64, 1)
    arbuf[224:240] = sums + pltpu.roll(sums, 32, 1)
    high, low = split(jnp.concatenate([tacc[8 * tap : 8 * tap + 8] for tap in range(9)], axis=1))
    by_read = jnp.sum(dot(high, k2t[...]) + dot(low, k2t[...]), axis=0, keepdims=True)
    arbuf[233:234, 0:32] = arbuf[233:234, 0:32] + by_read

    where_block = lane_block(8)
    rows = rowg[...]
    for b in range(4):
        vbuf[1, pl.ds(b, 8, stride=4), :] = jnp.where(where_block == 1, pltpu.roll(rows, (32 - 32 * b) % 128, 1) if b != 1 else rows, 0.0)
    all_of(arbuf.at[pl.ds(0, 128)], sems.at[0])
    all_of(cbuf, sems.at[3])
    all_of(cbuf, sems.at[2])
    own = colp[0:8]
    for m in range(1, REACH + 1):
        own = own + cbuf[m - 1]
    for b in range(4):
        vbuf[0, 8 * b : 8 * b + 8] = jnp.where(where_block == 0, pltpu.roll(own, (128 - 32 * b) % 128, 1) if b else own, 0.0)
    both = vbuf[0] + vbuf[1]
    high, low = split(both)
    by_feature = dot_t(jnp.concatenate([high, low], axis=0), jnp.concatenate([feat[...]] * 2, axis=0))
    arbuf[0:64] = by_feature[0:64, 0:128]
    arbuf[64:128] = by_feature[0:64, 128:256]

    def chunk(q):
        return pl.ds(pl.multiple_of(q * part, part), part)

    def send(source, place, at, device):
        pltpu.make_async_remote_copy(
            source, place, sems.at[at], sems.at[at + 1], device_id=(device,), device_id_type=MESH
        ).start()

    for s in range(1, side):
        send(arbuf.at[chunk(lax.rem(plane + s, side))], rsbuf.at[s - 1], 4, across(s))
    weights = jnp.concatenate([col_t[...], row_t[...]], axis=0)
    by_bin = dot(high[:, 0:64], weights) + dot(low[:, 0:64], weights)
    gbuf[256:288] = by_bin[:, 0:128]
    gbuf[288:320] = by_bin[:, 128:256]
    all_of(rsbuf, sems.at[5])
    total = arbuf[chunk(plane), :]
    for s in range(1, side):
        total = total + rsbuf[s - 1]
    mine[...] = total
    bbuf[pos] = total
    for s in range(1, SIDE):
        send(mine, bbuf.at[pos], 6, in_line(s))
    all_of(rsbuf, sems.at[4])
    all_of(bbuf.at[pl.ds(0, SIDE - 1)], sems.at[7])
    total = bbuf[0]
    for q in range(1, SIDE):
        total = total + bbuf[q]
    gbuf[chunk(plane), :] = total
    for s in range(1, side):
        send(gbuf.at[chunk(plane)], gbuf.at[chunk(plane)], 8, across(s))
    all_of(bbuf.at[pl.ds(0, SIDE - 1)], sems.at[6])
    all_of(rsbuf, sems.at[9])
    all_of(rsbuf, sems.at[8])
    red[...] = gbuf[...]


def finish_kernel(red, gfeat, grow, gcol, gone, gtwo, gread):
    gfeat[:, 0:128] = red[256:288]
    gfeat[:, 128:256] = red[288:320]
    gcol[:, 0:128] = red[0:32]
    gcol[:, 128:256] = red[64:96]
    grow[:, 0:128] = red[32:64]
    grow[:, 128:256] = red[96:128]
    for group in range(3):
        block = red[128 + 32 * group : 160 + 32 * group].T
        count = 128 if group < 2 else 32
        gone[128 * group : 128 * group + count] = block[0:count]
    by_channel = red[224:240].T
    read = red[320:321, 0:32]
    for tap in range(9):
        gtwo[32 * tap : 32 * tap + 32] = by_channel[0:32, tap : tap + 1] * read
    gread[...] = red[233:234, 0:32]


def shards(n, features, row_proj, col_proj, first_filter, second_filter, readout, target):
    side = n // SIDE
    part = TOTAL // side
    vmem = pl.BlockSpec(memory_space=pltpu.VMEM)

    def shape(*dims):
        return jax.ShapeDtypeStruct(dims, F32)

    def real(*dims):
        return pltpu.VMEM(dims, F32)

    def half(*dims):
        return pltpu.VMEM(dims, BF16)

    k1 = first_filter.reshape(9 * PAIR, PAIR)
    k2 = second_filter.reshape(9 * PAIR, PAIR)
    ro = readout.reshape(1, PAIR)
    row_t, col_t = row_proj.T, col_proj.T
    hbm = pl.BlockSpec(memory_space=pltpu.HBM)
    scratch = dict(
        feat=half(ROWS, 256), row_t=half(PAIR, 256), col_t=half(PAIR, 256), target=real(ROWS, 256), k1=half(288, PAIR), k2=half(288, PAIR),
        proj=real(32, 128), sbuf=real(16, 128), rbuf=real(AHEAD + 2, 16, 128), tlow=real(8, 256), thigh=real(8, 256),
        roww=real(24, 128), w1=half(1152, 256), wa=half(1152, 256), w2=real(72, 128), rol=real(8, 128),
        colr=real(LENGTH, 128), mk=pltpu.VMEM((LENGTH, 128), jnp.int32), ts=real(LENGTH, 128),
        act0=real(GROUPS + 2, LENGTH, 128), d0=real(GROUPS, LENGTH, 128),
        act1=real(GROUPS, LENGTH, 128), f1=real(GROUPS, LENGTH, 128), d1=real(GROUPS, LENGTH, 128),
        mis=real(GROUPS, LENGTH, 128), g1=real(GROUPS, LENGTH, 128),
        lhs=half(WIDE, 1152), lhs2=half(2 * WIDE, 1152), k2t=half(1152, PAIR), res=real(2 * WIDE, 256), qbuf=half(WIDE, 768), wq=half(768, 256),
        xall=half(8 * WIDE, 768), gall=half(8 * WIDE, 256), fg=real(256, 768), tacc=real(80, 128),
        colacc=real(LENGTH, 128), tiles=real(288, 256), colp=real(72, 128), rowg=real(8, 128),
        cbuf=real(REACH, 8, 128), vbuf=real(2, 32, 128), arbuf=real(256, 128), rsbuf=real(side - 1, part, 128),
        bbuf=real(SIDE, part, 128), mine=real(part, 128), gbuf=real(328, 128), loads=SEM((6,)), sems=SEM((10,)),
    )
    red = pl.pallas_call(
        functools.partial(step_kernel, n),
        out_shape=shape(328, 128),
        in_specs=[hbm] * 6 + [vmem],
        out_specs=vmem,
        scratch_shapes=list(scratch.values()),
        compiler_params=pltpu.CompilerParams(
            collective_id=0, has_side_effects=True, vmem_limit_bytes=60 * 1024 * 1024
        ),
        name="step",
    )(features, row_t, col_t, target, k1, k2, ro)

    gfeat, grow, gcol, gone, gtwo, gread = pl.pallas_call(
        finish_kernel,
        out_shape=(shape(ROWS, 256), shape(32, 256), shape(32, 256), shape(288, 32), shape(288, 32), shape(1, 32)),
        in_specs=[vmem],
        out_specs=(vmem,) * 6,
        compiler_params=pltpu.CompilerParams(vmem_limit_bytes=4 * 1024 * 1024),
        name="finish",
    )(red)
    return gfeat, grow.T, gcol.T, gone.reshape(3, 3, PAIR, PAIR), gtwo.reshape(3, 3, PAIR, PAIR), gread.reshape(PAIR)


def solution(mesh):
    n = mesh.shape["diag"]
    in_specs = (P("diag", None), P(), P(), P(), P(), P(), P("diag", None))
    out_specs = (P("diag", None), P(), P(), P(), P(), P())
    return jax.shard_map(
        functools.partial(shards, n), mesh=mesh, in_specs=in_specs, out_specs=out_specs, check_vma=False
    )
```

profile of v0, /device:TPU:1, one launch (start us, length us, event | category | flops | bytes accessed | tf_op | source)
XLA Modules:
  0.0 57.8 jit_solution(17165796228213587846)
XLA Ops:
  0.6 55.4 %step.1.red = f32[328,128]{1,0:T(8,128)} custom-call(bf16[32,256]{1,0:T(8,128)(2,1)} %feat_in.1, bf16[32,256]{1,0:T(8,128)(2,1)} %bitcast.12, bf16[32,256]{1,0:T(8,128)(2,1)} %bitcast.13, f32[32,256]{1,0:T(8,128)} %target_in.1, bf16[288,32]{1,0:T(8,128)(2,1)} %bitcast.10, bf16[288,32]{1,0:T(8,128)(2,1)} %bitcast.11, bf16[1,32]{1,0:T(2,128)(2,1)} %bitcast.14), custom_call_target="tpu_custom_call" | custom-call | tf_op jit(solution)/shard_map/step/pallas_call | solution.py:586
  56.0 0.0 copy-start
  56.1 0.9 %copy-done = f32[328,128]{1,0:T(8,128)S(1)} copy-done((f32[328,128]{1,0:T(8,128)S(1)}, f32[328,128]{1,0:T(8,128)}, u32[]{:S(2)}) %copy-start) | copy-done | bytes 167960
  57.0 0.9 %finish.1 = (f32[32,256]{1,0:T(8,128)}, f32[32,256]{1,0:T(8,128)}, f32[32,256]{1,0:T(8,128)}, f32[288,32]{1,0:T(8,128)}, f32[288,32]{1,0:T(8,128)}, /*index=5*/f32[1,32]{1,0:T(1,128)}) custom-call(f32[328,128]{1,0:T(8,128)S(1)} %copy-done), custom_call_target="tpu_custom_call" | custom-call | tf_op jit(solution)/shard_map/finish/pallas_call | solution.py:598
Async XLA Ops:
  56.0 0.9 %copy-start = (f32[328,128]{1,0:T(8,128)S(1)}, f32[328,128]{1,0:T(8,128)}, u32[]{:S(2)}) copy-start(f32[328,128]{1,0:T(8,128)} %step.1.red) | copy-start | bytes 503812
where the time goes:
time: 58 us; the launch traced here: 57.8 us
  Pallas kernels  56.3 us (97%)
  local copies, waits for them, and re-layouts  0.91 us (2%)
  between operations  0.65 us (1%)
    pallas_call x1, Pallas kernels, shards(): pl.pallas_call(functools.partial(step_kernel, n), out_shape=shape(328, 12...  55.4 us

commit v1 on v0

--- a/solution.py
+++ b/solution.py
@@ -37,11 +37,11 @@
     return lax.shift_right_logical(iota((rows, 128), 1), 5)
 
 
-def gelu(x, with_slope):
+def gelu(x):
     cubic = C1 * (x * x)
     s = 0.5 * jnp.tanh(x * (cubic + C0)) + 0.5
     value = x * s
-    slope = s + value * (1.0 - s) * (6.0 * cubic + 2.0 * C0) if with_slope else None
+    slope = s + value * (1.0 - s) * (6.0 * cubic + 2.0 * C0)
     return value.astype(BF16).astype(F32), slope
 
 
@@ -89,7 +89,7 @@
     n, feat_in, row_in, col_in, target_in, k1_in, k2_in, ro, red,
     feat, row_t, col_t, target, k1, k2,
     proj, sbuf, rbuf, tlow, thigh, roww, w1, wa, w2, rol, colr, mk, ts, act0, d0, act1, f1, d1, mis, g1,
-    lhs, lhs2, k2t, res, qbuf, wq, xall, gall, fg, tacc, colacc, tiles, colp, rowg, cbuf, vbuf, arbuf, rsbuf, bbuf, mine, gbuf,
+    lhs, lhs2, k2t, res, qbuf, wq, xall, gall, galt, fg, tacc, colacc, tiles, colp, rowg, cbuf, vbuf, arbuf, rsbuf, bbuf, mine, gbuf,
     loads, sems,
 ):
     me = lax.axis_index("diag")
@@ -192,8 +192,7 @@
 
     tiles[...] = dot(k1[...], rep8)
     build(w1, 1)
-    for tap in range(9):
-        tiles[32 * tap : 32 * tap + 32] = dot_t(k1[32 * tap : 32 * tap + 32], rep8)
+    tiles[...] = dot_t(jnp.concatenate([k1[32 * tap : 32 * tap + 32] for tap in range(9)], axis=1), rep8)
     build(wa, -1)
     ro8 = jnp.broadcast_to(ro[...].astype(F32), (8, PAIR)).astype(BF16)
     rol[...] = dot(ro8, repeater(128))
@@ -252,7 +251,7 @@
         ends = jnp.where(left, buffer[index + 3, pl.ds(row, WIDE), :], buffer[index, pl.ds(row, WIDE), :])
         return ends, buffer[index + 1, pl.ds(row, WIDE), :], buffer[index + 2, pl.ds(row, WIDE), :]
 
-    def make_field(with_slope, v):
+    def make_field(v):
         base = pl.multiple_of(8 * v, 8)
         for h in range(2):
             u = 2 * v + h
@@ -262,10 +261,9 @@
                 row = base + PAD + CHUNK * ch
                 mask = mask_at(u, row, CHUNK)
                 x = jnp.where(mask, row_here + colr[pl.ds(row, CHUNK), :], 0.0)
-                act, slope = gelu(x, with_slope)
+                act, slope = gelu(x)
                 act0[u + 1, pl.ds(row, CHUNK), :] = act
-                if with_slope:
-                    d0[u, pl.ds(row, CHUNK), :] = jnp.where(mask, slope, 0.0)
+                d0[u, pl.ds(row, CHUNK), :] = jnp.where(mask, slope, 0.0)
 
     def conv_operand(v):
         base = pl.multiple_of(8 * v, 8)
@@ -276,7 +274,7 @@
     def conv():
         res[0:WIDE] = dot(lhs[...], w1[...])
 
-    def conv_result(with_slope, v):
+    def conv_result(v):
         base = pl.multiple_of(8 * v, 8)
         for h in range(2):
             u = 2 * v + h
@@ -288,29 +286,24 @@
                 added = res[CHUNK * ch : CHUNK * ch + CHUNK, 128 * h : 128 * h + 128]
                 mask = mask_at(u, row, CHUNK)
                 x = jnp.where(mask, (row_here + colr[pl.ds(row, CHUNK), :]) + added, 0.0)
-                act, slope = gelu(x, with_slope)
+                act, slope = gelu(x)
                 act1[u, pl.ds(row, CHUNK), :] = act
                 f1[u, pl.ds(row, CHUNK), :] = x
-                if with_slope:
-                    d1[u, pl.ds(row, CHUNK), :] = jnp.where(mask, slope, 0.0)
-
-    make_field(False, 0)
-    make_field(True, 1)
-    conv_operand(0)
-    make_field(True, 2)
-    conv()
-
-    def first_conv(with_field, v, carry):
+                d1[u, pl.ds(row, CHUNK), :] = jnp.where(mask, slope, 0.0)
+
+    def fields(v, carry):
+        make_field(v)
+        return carry
+
+    lax.fori_loop(0, GROUPS // 2, fields, 0)
+
+    def first_conv(v, carry):
         conv_operand(v)
-        conv_result(True, v - 1)
-        if with_field:
-            make_field(True, v + 2)
         conv()
-        return carry
-
-    lax.fori_loop(1, 5, functools.partial(first_conv, True), 0)
-    lax.fori_loop(5, 7, functools.partial(first_conv, False), 0)
-    conv_result(False, 6)
+        conv_result(v)
+        return carry
+
+    lax.fori_loop(0, GROUPS // 2, first_conv, 0)
 
     def make_misfit(w, carry):
         base = pl.multiple_of(8 * w, 8)
@@ -412,22 +405,17 @@
             for q in range(3):
                 row = base + PAD + 2 * (q - 1)
                 ends = jnp.where(left, act0[u + 2, pl.ds(row, WIDE), :], act0[u, pl.ds(row, WIDE), :])
-                xall[pl.ds(at, WIDE), 256 * q : 256 * q + 128] = ends.astype(BF16)
-                xall[pl.ds(at, WIDE), 256 * q + 128 : 256 * q + 256] = act0[u + 1, pl.ds(row, WIDE), :].astype(BF16)
-
-    adjoint_operand(0)
-    collect(0)
-    adjoint()
+                xall[q, pl.ds(at, WIDE), 0:128] = ends.astype(BF16)
+                xall[q, pl.ds(at, WIDE), 128:256] = act0[u + 1, pl.ds(row, WIDE), :].astype(BF16)
 
     def first_adjoint(w, carry):
         adjoint_operand(w)
-        adjoint_result(w - 1)
         collect(w)
         adjoint()
-        return carry
-
-    lax.fori_loop(1, 4, first_adjoint, 0)
-    adjoint_result(3)
+        adjoint_result(w)
+        return carry
+
+    lax.fori_loop(0, 4, first_adjoint, 0)
 
     where_block = lane_block(8)
     for m in range(REACH + 1):
@@ -449,7 +437,13 @@
     for copy in columns:
         copy.start()
 
-    fg[...] = dot_t(gall[...], xall[...])
+    galt[...] = gall[...].T
+
+    def by_column_tap(q, carry):
+        fg[q] = dot(galt[...], xall[q])
+        return carry
+
+    lax.fori_loop(0, 3, by_column_tap, 0)
 
     where_block = lane_block(32)
     for group in range(3):
@@ -462,8 +456,8 @@
             value = jnp.zeros((32, 128), F32)
             for b in range(4):
                 source = b + 2 * p
-                lanes = 256 * q + (128 if 0 <= source < 4 else 0)
-                both = fg[32 * b : 32 * b + 32, lanes : lanes + 128] + fg[128 + 32 * b : 160 + 32 * b, lanes : lanes + 128]
+                lanes = slice(128, 256) if 0 <= source < 4 else slice(0, 128)
+                both = fg[q, 32 * b : 32 * b + 32, lanes] + fg[q, 128 + 32 * b : 160 + 32 * b, lanes]
                 value = value + jnp.where(where_block == source % 4, both, 0.0)
             value = value + pltpu.roll(value, 64, 1)
             value = value + pltpu.roll(value, 32, 1)
@@ -504,8 +498,14 @@
             source, place, sems.at[at], sems.at[at + 1], device_id=(device,), device_id_type=MESH
         ).start()
 
-    for s in range(1, side):
-        send(arbuf.at[chunk(lax.rem(plane + s, side))], rsbuf.at[s - 1], 4, across(s))
+    def each(count, action):
+        def step(s, carry):
+            action(s)
+            return carry
+
+        lax.fori_loop(1, count, step, 0)
+
+    each(side, lambda s: send(arbuf.at[chunk(lax.rem(plane + s, side))], rsbuf.at[s - 1], 4, across(s)))
     weights = jnp.concatenate([col_t[...], row_t[...]], axis=0)
     by_bin = dot(high[:, 0:64], weights) + dot(low[:, 0:64], weights)
     gbuf[256:288] = by_bin[:, 0:128]
@@ -516,16 +516,14 @@
         total = total + rsbuf[s - 1]
     mine[...] = total
     bbuf[pos] = total
-    for s in range(1, SIDE):
-        send(mine, bbuf.at[pos], 6, in_line(s))
+    each(SIDE, lambda s: send(mine, bbuf.at[pos], 6, in_line(s)))
     all_of(rsbuf, sems.at[4])
     all_of(bbuf.at[pl.ds(0, SIDE - 1)], sems.at[7])
     total = bbuf[0]
     for q in range(1, SIDE):
         total = total + bbuf[q]
     gbuf[chunk(plane), :] = total
-    for s in range(1, side):
-        send(gbuf.at[chunk(plane)], gbuf.at[chunk(plane)], 8, across(s))
+    each(side, lambda s: send(gbuf.at[chunk(plane)], gbuf.at[chunk(plane)], 8, across(s)))
     all_of(bbuf.at[pl.ds(0, SIDE - 1)], sems.at[6])
     all_of(rsbuf, sems.at[9])
     all_of(rsbuf, sems.at[8])
@@ -578,7 +576,7 @@
         act1=real(GROUPS, LENGTH, 128), f1=real(GROUPS, LENGTH, 128), d1=real(GROUPS, LENGTH, 128),
         mis=real(GROUPS, LENGTH, 128), g1=real(GROUPS, LENGTH, 128),
         lhs=half(WIDE, 1152), lhs2=half(2 * WIDE, 1152), k2t=half(1152, PAIR), res=real(2 * WIDE, 256), qbuf=half(WIDE, 768), wq=half(768, 256),
-        xall=half(8 * WIDE, 768), gall=half(8 * WIDE, 256), fg=real(256, 768), tacc=real(80, 128),
+        xall=half(3, 8 * WIDE, 256), gall=half(8 * WIDE, 256), galt=half(256, 8 * WIDE), fg=real(3, 256, 256), tacc=real(80, 128),
         colacc=real(LENGTH, 128), tiles=real(288, 256), colp=real(72, 128), rowg=real(8, 128),
         cbuf=real(REACH, 8, 128), vbuf=real(2, 32, 128), arbuf=real(256, 128), rsbuf=real(side - 1, part, 128),
         bbuf=real(SIDE, part, 128), mine=real(part, 128), gbuf=real(328, 128), loads=SEM((6,)), sems=SEM((10,)),

time: 58 us -> 58.8 us (1.014)
  Pallas kernels: 56.3 us -> 57 us
    pallas_call x1, Pallas kernels: 55.4 us -> 56.1 us  [shards(): pl.pallas_call(functools.partial(step_kernel, n), out_shape=shape(328, 12...]
where the time goes in v1:
time: 58.8 us; the launch traced here: 58.6 us
  Pallas kernels  57 us (97%)
  local copies, waits for them, and re-layouts  0.91 us (2%)
  between operations  0.65 us (1%)
    pallas_call x1, Pallas kernels, shards(): pl.pallas_call(functools.partial(step_kernel, n), out_shape=shape(328, 12...  56.1 us

profile of v1, /device:TPU:1, one launch (start us, length us, event | category | flops | bytes accessed | tf_op | source)
XLA Modules:
  0.0 58.6 jit_solution(11371268378966188529)
XLA Ops:
  0.6 56.1 %step.1.red = f32[328,128]{1,0:T(8,128)} custom-call(bf16[32,256]{1,0:T(8,128)(2,1)} %feat_in.1, bf16[32,256]{1,0:T(8,128)(2,1)} %bitcast.12, bf16[32,256]{1,0:T(8,128)(2,1)} %bitcast.13, f32[32,256]{1,0:T(8,128)} %target_in.1, bf16[288,32]{1,0:T(8,128)(2,1)} %bitcast.10, bf16[288,32]{1,0:T(8,128)(2,1)} %bitcast.11, bf16[1,32]{1,0:T(2,128)(2,1)} %bitcast.14), custom_call_target="tpu_custom_call" | custom-call | tf_op jit(solution)/shard_map/step/pallas_call | solution.py:584
  56.8 0.0 copy-start
  56.8 0.9 %copy-done = f32[328,128]{1,0:T(8,128)S(1)} copy-done((f32[328,128]{1,0:T(8,128)S(1)}, f32[328,128]{1,0:T(8,128)}, u32[]{:S(2)}) %copy-start) | copy-done | bytes 167960
  57.7 0.9 %finish.1 = (f32[32,256]{1,0:T(8,128)}, f32[32,256]{1,0:T(8,128)}, f32[32,256]{1,0:T(8,128)}, f32[288,32]{1,0:T(8,128)}, f32[288,32]{1,0:T(8,128)}, /*index=5*/f32[1,32]{1,0:T(1,128)}) custom-call(f32[328,128]{1,0:T(8,128)S(1)} %copy-done), custom_call_target="tpu_custom_call" | custom-call | tf_op jit(solution)/shard_map/finish/pallas_call | solution.py:596
Async XLA Ops:
  56.8 0.9 %copy-start = (f32[328,128]{1,0:T(8,128)S(1)}, f32[328,128]{1,0:T(8,128)}, u32[]{:S(2)}) copy-start(f32[328,128]{1,0:T(8,128)} %step.1.red) | copy-start | bytes 503812

commit v2 on v0

--- a/solution.py
+++ b/solution.py
@@ -150,15 +150,15 @@
     greeted = jnp.maximum(SIDE - AHEAD - 1 - pos, 0) + jnp.maximum(pos - AHEAD, 0)
     pl.semaphore_wait(barrier, 2 * AHEAD + greeted + side - 1)
     gathers = []
-    for slot, step in ((0, 1), (2, -1)):
-        gathers.append(
-            pltpu.make_async_remote_copy(sbuf, rbuf.at[slot], sems.at[0], sems.at[1], device_id=(dev(step),), device_id_type=MESH)
-        )
-    for m in range(3, AHEAD + 2):
+    for m in range(AHEAD + 1, 2, -1):
         gathers.append(
             pltpu.make_async_remote_copy(
                 sbuf.at[pl.ds(0, 8)], rbuf.at[m, pl.ds(0, 8)], sems.at[0], sems.at[1], device_id=(dev(1 - m),), device_id_type=MESH
             )
+        )
+    for slot, step in ((0, 1), (2, -1)):
+        gathers.append(
+            pltpu.make_async_remote_copy(sbuf, rbuf.at[slot], sems.at[0], sems.at[1], device_id=(dev(step),), device_id_type=MESH)
         )
     gathers.append(
         pltpu.make_async_remote_copy(
@@ -192,8 +192,7 @@
 
     tiles[...] = dot(k1[...], rep8)
     build(w1, 1)
-    for tap in range(9):
-        tiles[32 * tap : 32 * tap + 32] = dot_t(k1[32 * tap : 32 * tap + 32], rep8)
+    tiles[...] = dot_t(jnp.concatenate([k1[32 * tap : 32 * tap + 32] for tap in range(9)], axis=1), rep8)
     build(wa, -1)
     ro8 = jnp.broadcast_to(ro[...].astype(F32), (8, PAIR)).astype(BF16)
     rol[...] = dot(ro8, repeater(128))
@@ -229,12 +228,6 @@
     roww[0:8] = rbuf[0, 8:16]
     roww[8:16] = row_c
     roww[16:24] = rbuf[2, 8:16]
-    wide = jnp.concatenate([tlow[...], target[...], thigh[...]], axis=0)
-    wide = jnp.concatenate([wide, jnp.zeros((48, 128), F32)], axis=1)
-    wide = jnp.concatenate([wide, jnp.zeros((80, 384), F32)], axis=0)
-    sheared = pltpu.roll(wide, 0, 1, stride=1, stride_axis=0)
-    ts[4 + PAD : 4 + PAD + 312] = sheared.T[0:312]
-
     def first_column(u):
         return pl.multiple_of(8 * lax.shift_right_logical(u, 1), 8)
 
@@ -297,6 +290,11 @@
     make_field(False, 0)
     make_field(True, 1)
     conv_operand(0)
+    wide = jnp.concatenate([tlow[...], target[...], thigh[...]], axis=0)
+    wide = jnp.concatenate([wide, jnp.zeros((48, 128), F32)], axis=1)
+    wide = jnp.concatenate([wide, jnp.zeros((80, 384), F32)], axis=0)
+    sheared = pltpu.roll(wide, 0, 1, stride=1, stride_axis=0)
+    ts[4 + PAD : 4 + PAD + 312] = sheared.T[0:312]
     make_field(True, 2)
     conv()
 
@@ -478,6 +476,24 @@
     by_read = jnp.sum(dot(high, k2t[...]) + dot(low, k2t[...]), axis=0, keepdims=True)
     arbuf[233:234, 0:32] = arbuf[233:234, 0:32] + by_read
 
+    def chunk(q):
+        return pl.ds(pl.multiple_of(q * part, part), part)
+
+    def send(source, place, at, device):
+        pltpu.make_async_remote_copy(
+            source, place, sems.at[at], sems.at[at + 1], device_id=(device,), device_id_type=MESH
+        ).start()
+
+    def scatter(begin, end):
+        for q in range(begin, end):
+            s = lax.rem(q - plane + side, side)
+
+            @pl.when(s > 0)
+            def _():
+                send(arbuf.at[pl.ds(q * part, part)], rsbuf.at[s - 1], 4, across(s))
+
+    scatter(side // 2, side)
+
     where_block = lane_block(8)
     rows = rowg[...]
     for b in range(4):
@@ -496,20 +512,13 @@
     arbuf[0:64] = by_feature[0:64, 0:128]
     arbuf[64:128] = by_feature[0:64, 128:256]
 
-    def chunk(q):
-        return pl.ds(pl.multiple_of(q * part, part), part)
-
-    def send(source, place, at, device):
-        pltpu.make_async_remote_copy(
-            source, place, sems.at[at], sems.at[at + 1], device_id=(device,), device_id_type=MESH
-        ).start()
-
-    for s in range(1, side):
-        send(arbuf.at[chunk(lax.rem(plane + s, side))], rsbuf.at[s - 1], 4, across(s))
+    scatter(0, side // 2)
     weights = jnp.concatenate([col_t[...], row_t[...]], axis=0)
     by_bin = dot(high[:, 0:64], weights) + dot(low[:, 0:64], weights)
     gbuf[256:288] = by_bin[:, 0:128]
     gbuf[288:320] = by_bin[:, 128:256]
+    keep = pltpu.make_async_copy(gbuf.at[pl.ds(256, 72)], red.at[pl.ds(256, 72)], loads.at[6])
+    keep.start()
     all_of(rsbuf, sems.at[5])
     total = arbuf[chunk(plane), :]
     for s in range(1, side):
@@ -525,11 +534,14 @@
         total = total + bbuf[q]
     gbuf[chunk(plane), :] = total
     for s in range(1, side):
-        send(gbuf.at[chunk(plane)], gbuf.at[chunk(plane)], 8, across(s))
+        send(gbuf.at[chunk(plane)], red.at[chunk(plane)], 8, across(s))
+    place = pltpu.make_async_copy(gbuf.at[chunk(plane)], red.at[chunk(plane)], loads.at[7])
+    place.start()
     all_of(bbuf.at[pl.ds(0, SIDE - 1)], sems.at[6])
     all_of(rsbuf, sems.at[9])
     all_of(rsbuf, sems.at[8])
-    red[...] = gbuf[...]
+    keep.wait()
+    place.wait()
 
 
 def finish_kernel(red, gfeat, grow, gcol, gone, gtwo, gread):
@@ -581,13 +593,13 @@
         xall=half(8 * WIDE, 768), gall=half(8 * WIDE, 256), fg=real(256, 768), tacc=real(80, 128),
         colacc=real(LENGTH, 128), tiles=real(288, 256), colp=real(72, 128), rowg=real(8, 128),
         cbuf=real(REACH, 8, 128), vbuf=real(2, 32, 128), arbuf=real(256, 128), rsbuf=real(side - 1, part, 128),
-        bbuf=real(SIDE, part, 128), mine=real(part, 128), gbuf=real(328, 128), loads=SEM((6,)), sems=SEM((10,)),
+        bbuf=real(SIDE, part, 128), mine=real(part, 128), gbuf=real(328, 128), loads=SEM((8,)), sems=SEM((10,)),
     )
     red = pl.pallas_call(
         functools.partial(step_kernel, n),
         out_shape=shape(328, 128),
         in_specs=[hbm] * 6 + [vmem],
-        out_specs=vmem,
+        out_specs=hbm,
         scratch_shapes=list(scratch.values()),
         compiler_params=pltpu.CompilerParams(
             collective_id=0, has_side_effects=True, vmem_limit_bytes=60 * 1024 * 1024

time: 58 us -> 55.6 us (0.959)
  Pallas kernels: 56.3 us -> 53.9 us
    pallas_call x1, Pallas kernels: 55.4 us -> 53 us  [shards(): pl.pallas_call(functools.partial(step_kernel, n), out_shape=shape(328, 12...]
where the time goes in v2:
time: 55.6 us; the launch traced here: 55.4 us
  Pallas kernels  53.9 us (97%)
  local copies, waits for them, and re-layouts  0.91 us (2%)
  between operations  0.65 us (1%)
    pallas_call x1, Pallas kernels, shards(): pl.pallas_call(functools.partial(step_kernel, n), out_shape=shape(328, 12...  53 us

profile of v2, /device:TPU:1, one launch (start us, length us, event | category | flops | bytes accessed | tf_op | source)
XLA Modules:
  0.0 55.4 jit_solution(18055175521766423919)
XLA Ops:
  0.6 53.0 %step.1.red = f32[328,128]{1,0:T(8,128)} custom-call(bf16[32,256]{1,0:T(8,128)(2,1)} %feat_in.1, bf16[32,256]{1,0:T(8,128)(2,1)} %bitcast.12, bf16[32,256]{1,0:T(8,128)(2,1)} %bitcast.13, f32[32,256]{1,0:T(8,128)} %target_in.1, bf16[288,32]{1,0:T(8,128)(2,1)} %bitcast.10, bf16[288,32]{1,0:T(8,128)(2,1)} %bitcast.11, bf16[1,32]{1,0:T(2,128)(2,1)} %bitcast.14), custom_call_target="tpu_custom_call" | custom-call | tf_op jit(solution)/shard_map/step/pallas_call | solution.py:598
  53.6 0.0 copy-start
  53.6 0.9 %copy-done = f32[328,128]{1,0:T(8,128)S(1)} copy-done((f32[328,128]{1,0:T(8,128)S(1)}, f32[328,128]{1,0:T(8,128)}, u32[]{:S(2)}) %copy-start) | copy-done | bytes 167960
  54.5 0.9 %finish.1 = (f32[32,256]{1,0:T(8,128)}, f32[32,256]{1,0:T(8,128)}, f32[32,256]{1,0:T(8,128)}, f32[288,32]{1,0:T(8,128)}, f32[288,32]{1,0:T(8,128)}, /*index=5*/f32[1,32]{1,0:T(1,128)}) custom-call(f32[328,128]{1,0:T(8,128)S(1)} %copy-done), custom_call_target="tpu_custom_call" | custom-call | tf_op jit(solution)/shard_map/finish/pallas_call | solution.py:610
Async XLA Ops:
  53.6 0.9 %copy-start = (f32[328,128]{1,0:T(8,128)S(1)}, f32[328,128]{1,0:T(8,128)}, u32[]{:S(2)}) copy-start(f32[328,128]{1,0:T(8,128)} %step.1.red) | copy-start | bytes 503812

commit v3 on v2

--- a/solution.py
+++ b/solution.py
@@ -312,16 +312,19 @@
 
     def make_misfit(w, carry):
         base = pl.multiple_of(8 * w, 8)
-        for at, count in ((0, 96), (96, 96), (192, 80)):
+        for at, count in ((0, 48), (48, 48), (96, 48), (144, 48), (192, 48), (240, 32)):
             row = base + PAD + at
+            values = [rol[0:1] * f1[2 * w + 1 + h, pl.ds(row, count), :] for h in range(2)]
+            for g in range(4):
+                for q in range(3):
+                    act = act1[2 * w + g, pl.ds(row + 4 * (q - 1), count), :]
+                    for h in range(2):
+                        p = g - h
+                        if 0 <= p < 3:
+                            tap = 3 * p + q
+                            values[h] = values[h] + w2[8 * tap : 8 * tap + 1] * act
             for h in range(2):
-                u = 2 * w + 1 + h
-                value = rol[0:1] * f1[u, pl.ds(row, count), :]
-                for p in range(3):
-                    for q in range(3):
-                        tap = 3 * p + q
-                        value = value + w2[8 * tap : 8 * tap + 1] * act1[u + p - 1, pl.ds(row + 4 * (q - 1), count), :]
-                high, low = split(value)
+                high, low = split(values[h])
                 qbuf[at : at + count, 128 * h : 128 * h + 128] = high
                 qbuf[at : at + count, 256 + 128 * h : 384 + 128 * h] = low
             high, low = split(ts[pl.ds(row, count), :])
@@ -343,33 +346,42 @@
 
     lax.fori_loop(0, 6, make_misfit, 0)
 
-    def make_cotangent(u, carry):
-        base = first_column(u)
-        clear_sides(g1, u, base)
-        sums = [None] * 10
-        for ch in range(3):
-            row = base + PAD + CHUNK * ch
-            act = act1[u, pl.ds(row, CHUNK), :]
-            back = None
-            for p in range(3):
+    def make_cotangent(v, carry):
+        base = pl.multiple_of(8 * v, 8)
+        sums = [[None] * 10 for h in range(2)]
+        for h in range(2):
+            clear_sides(g1, 2 * v + h, base)
+        for ch in range(SPAN // 24):
+            row = base + PAD + 24 * ch
+            acts = [act1[2 * v + h, pl.ds(row, 24), :] for h in range(2)]
+            backs = [None, None]
+            centers = [None, None]
+            for g in range(4):
                 for q in range(3):
-                    tap = 3 * p + q
-                    m = mis[u - (p - 1), pl.ds(row - 4 * (q - 1), CHUNK), :]
-                    term = w2[8 * tap : 8 * tap + 1] * m
-                    back = term if back is None else back + term
-                    part = fold(act * m)
-                    sums[tap] = part if sums[tap] is None else sums[tap] + part
-            m = mis[u, pl.ds(row, CHUNK), :]
-            part = fold(m * f1[u, pl.ds(row, CHUNK), :])
-            sums[9] = part if sums[9] is None else sums[9] + part
-            g1[u, pl.ds(row, CHUNK), :] = rol[0:1] * m + d1[u, pl.ds(row, CHUNK), :] * back
+                    m = mis[2 * v - 1 + g, pl.ds(row - 4 * (q - 1), 24), :]
+                    for h in range(2):
+                        p = h + 2 - g
+                        if 0 <= p < 3:
+                            tap = 3 * p + q
+                            term = w2[8 * tap : 8 * tap + 1] * m
+                            backs[h] = term if backs[h] is None else backs[h] + term
+                            part_sum = fold(acts[h] * m)
+                            sums[h][tap] = part_sum if sums[h][tap] is None else sums[h][tap] + part_sum
+                            if tap == 4:
+                                centers[h] = m
+            for h in range(2):
+                u = 2 * v + h
+                part_sum = fold(centers[h] * f1[u, pl.ds(row, 24), :])
+                sums[h][9] = part_sum if sums[h][9] is None else sums[h][9] + part_sum
+                g1[u, pl.ds(row, 24), :] = rol[0:1] * centers[h] + d1[u, pl.ds(row, 24), :] * backs[h]
         for tap in range(10):
-            source = u - (tap // 3 - 1) if tap < 9 else u
-            own = jnp.logical_and(source >= FIRST_OWN, source <= LAST_OWN)
-            tacc[8 * tap : 8 * tap + 8] += jnp.where(own, sums[tap], 0.0)
+            for h in range(2):
+                source = 2 * v + h - (tap // 3 - 1) if tap < 9 else 2 * v + h
+                own = jnp.logical_and(source >= FIRST_OWN, source <= LAST_OWN)
+                tacc[8 * tap : 8 * tap + 8] += jnp.where(own, sums[h][tap], 0.0)
         return carry
 
-    lax.fori_loop(2, GROUPS - 2, make_cotangent, 0)
+    lax.fori_loop(1, 6, make_cotangent, 0)
 
     def adjoint_operand(w):
         base = pl.multiple_of(8 * w + 8, 8)

time: 55.6 us -> 55.3 us (level)
  no operation moved by 1% of the time
where the time goes in v3:
time: 55.3 us; the launch traced here: 55.1 us
  Pallas kernels  53.6 us (97%)
  local copies, waits for them, and re-layouts  0.91 us (2%)
  between operations  0.65 us (1%)
    pallas_call x1, Pallas kernels, shards(): pl.pallas_call(functools.partial(step_kernel, n), out_shape=shape(328, 12...  52.7 us

profile of v3, /device:TPU:1, one launch (start us, length us, event | category | flops | bytes accessed | tf_op | source)
XLA Modules:
  0.0 55.1 jit_solution(9545907190146996374)
XLA Ops:
  0.6 52.7 %step.1.red = f32[328,128]{1,0:T(8,128)} custom-call(bf16[32,256]{1,0:T(8,128)(2,1)} %feat_in.1, bf16[32,256]{1,0:T(8,128)(2,1)} %bitcast.12, bf16[32,256]{1,0:T(8,128)(2,1)} %bitcast.13, f32[32,256]{1,0:T(8,128)} %target_in.1, bf16[288,32]{1,0:T(8,128)(2,1)} %bitcast.10, bf16[288,32]{1,0:T(8,128)(2,1)} %bitcast.11, bf16[1,32]{1,0:T(2,128)(2,1)} %bitcast.14), custom_call_target="tpu_custom_call" | custom-call | tf_op jit(solution)/shard_map/step/pallas_call | solution.py:610
  53.3 0.0 copy-start
  53.3 0.9 %copy-done = f32[328,128]{1,0:T(8,128)S(1)} copy-done((f32[328,128]{1,0:T(8,128)S(1)}, f32[328,128]{1,0:T(8,128)}, u32[]{:S(2)}) %copy-start) | copy-done | bytes 167960
  54.2 0.9 %finish.1 = (f32[32,256]{1,0:T(8,128)}, f32[32,256]{1,0:T(8,128)}, f32[32,256]{1,0:T(8,128)}, f32[288,32]{1,0:T(8,128)}, f32[288,32]{1,0:T(8,128)}, /*index=5*/f32[1,32]{1,0:T(1,128)}) custom-call(f32[328,128]{1,0:T(8,128)S(1)} %copy-done), custom_call_target="tpu_custom_call" | custom-call | tf_op jit(solution)/shard_map/finish/pallas_call | solution.py:622
Async XLA Ops:
  53.3 0.9 %copy-start = (f32[328,128]{1,0:T(8,128)S(1)}, f32[328,128]{1,0:T(8,128)}, u32[]{:S(2)}) copy-start(f32[328,128]{1,0:T(8,128)} %step.1.red) | copy-start | bytes 503812

commit v4 on v3

--- a/solution.py
+++ b/solution.py
@@ -25,6 +25,7 @@
 C0 = math.sqrt(2.0 / math.pi)
 C1 = C0 * 0.044715
 SIDE = 16
+LINE = 8
 TOTAL = 256
 SEM = pltpu.SemaphoreType.DMA
 
@@ -89,7 +90,7 @@
     n, feat_in, row_in, col_in, target_in, k1_in, k2_in, ro, red,
     feat, row_t, col_t, target, k1, k2,
     proj, sbuf, rbuf, tlow, thigh, roww, w1, wa, w2, rol, colr, mk, ts, act0, d0, act1, f1, d1, mis, g1,
-    lhs, lhs2, k2t, res, qbuf, wq, xall, gall, fg, tacc, colacc, tiles, colp, rowg, cbuf, vbuf, arbuf, rsbuf, bbuf, mine, gbuf,
+    lhs, lhs2, k2t, res, qbuf, wq, xall, gall, fg, tacc, colacc, tiles, colp, rowg, cbuf, vbuf, arbuf, rsbuf, bbuf, mine, other, chip, gbuf,
     loads, sems,
 ):
     me = lax.axis_index("diag")
@@ -98,12 +99,10 @@
     part = TOTAL // side
     pos = lax.rem(me, SIDE)
     plane = lax.div(me, SIDE)
+    depth = lax.div(pos, 2)
 
     def dev(step):
         return lax.rem(me + step + n, n)
-
-    def in_line(s):
-        return me - pos + lax.rem(pos + s, SIDE)
 
     def across(s):
         return lax.rem(plane + s, side) * SIDE + pos
@@ -536,20 +535,25 @@
     for s in range(1, side):
         total = total + rsbuf[s - 1]
     mine[...] = total
-    bbuf[pos] = total
-    for s in range(1, SIDE):
-        send(mine, bbuf.at[pos], 6, in_line(s))
+    send(mine, other, 10, me + 1 - 2 * lax.rem(me, 2))
     all_of(rsbuf, sems.at[4])
-    all_of(bbuf.at[pl.ds(0, SIDE - 1)], sems.at[7])
+    all_of(other, sems.at[11])
+    total = total + other[...]
+    chip[...] = total
+    bbuf[depth] = total
+    for s in range(1, LINE):
+        send(chip, bbuf.at[depth], 6, me + 2 * (lax.rem(depth + s, LINE) - depth))
+    all_of(other, sems.at[10])
+    all_of(bbuf.at[pl.ds(0, LINE - 1)], sems.at[7])
     total = bbuf[0]
-    for q in range(1, SIDE):
+    for q in range(1, LINE):
         total = total + bbuf[q]
     gbuf[chunk(plane), :] = total
     for s in range(1, side):
         send(gbuf.at[chunk(plane)], red.at[chunk(plane)], 8, across(s))
     place = pltpu.make_async_copy(gbuf.at[chunk(plane)], red.at[chunk(plane)], loads.at[7])
     place.start()
-    all_of(bbuf.at[pl.ds(0, SIDE - 1)], sems.at[6])
+    all_of(bbuf.at[pl.ds(0, LINE - 1)], sems.at[6])
     all_of(rsbuf, sems.at[9])
     all_of(rsbuf, sems.at[8])
     keep.wait()
@@ -605,7 +609,7 @@
         xall=half(8 * WIDE, 768), gall=half(8 * WIDE, 256), fg=real(256, 768), tacc=real(80, 128),
         colacc=real(LENGTH, 128), tiles=real(288, 256), colp=real(72, 128), rowg=real(8, 128),
         cbuf=real(REACH, 8, 128), vbuf=real(2, 32, 128), arbuf=real(256, 128), rsbuf=real(side - 1, part, 128),
-        bbuf=real(SIDE, part, 128), mine=real(part, 128), gbuf=real(328, 128), loads=SEM((8,)), sems=SEM((10,)),
+        bbuf=real(LINE, part, 128), mine=real(part, 128), other=real(part, 128), chip=real(part, 128), gbuf=real(328, 128), loads=SEM((8,)), sems=SEM((12,)),
     )
     red = pl.pallas_call(
         functools.partial(step_kernel, n),

time: 55.3 us -> 55.3 us (level)
  no operation moved by 1% of the time
where the time goes in v4:
time: 55.3 us; the launch traced here: 55.1 us
  Pallas kernels  53.6 us (97%)
  local copies, waits for them, and re-layouts  0.91 us (2%)
  between operations  0.65 us (1%)
    pallas_call x1, Pallas kernels, shards(): pl.pallas_call(functools.partial(step_kernel, n), out_shape=shape(328, 12...  52.7 us

profile of v4, /device:TPU:1, one launch (start us, length us, event | category | flops | bytes accessed | tf_op | source)
XLA Modules:
  0.0 55.1 jit_solution(18401043616086047054)
XLA Ops:
  0.6 52.7 %step.1.red = f32[328,128]{1,0:T(8,128)} custom-call(bf16[32,256]{1,0:T(8,128)(2,1)} %feat_in.1, bf16[32,256]{1,0:T(8,128)(2,1)} %bitcast.12, bf16[32,256]{1,0:T(8,128)(2,1)} %bitcast.13, f32[32,256]{1,0:T(8,128)} %target_in.1, bf16[288,32]{1,0:T(8,128)(2,1)} %bitcast.10, bf16[288,32]{1,0:T(8,128)(2,1)} %bitcast.11, bf16[1,32]{1,0:T(2,128)(2,1)} %bitcast.14), custom_call_target="tpu_custom_call" | custom-call | tf_op jit(solution)/shard_map/step/pallas_call | solution.py:614
  53.3 0.0 copy-start
  53.3 0.9 %copy-done = f32[328,128]{1,0:T(8,128)S(1)} copy-done((f32[328,128]{1,0:T(8,128)S(1)}, f32[328,128]{1,0:T(8,128)}, u32[]{:S(2)}) %copy-start) | copy-done | bytes 167960
  54.2 0.9 %finish.1 = (f32[32,256]{1,0:T(8,128)}, f32[32,256]{1,0:T(8,128)}, f32[32,256]{1,0:T(8,128)}, f32[288,32]{1,0:T(8,128)}, f32[288,32]{1,0:T(8,128)}, /*index=5*/f32[1,32]{1,0:T(1,128)}) custom-call(f32[328,128]{1,0:T(8,128)S(1)} %copy-done), custom_call_target="tpu_custom_call" | custom-call | tf_op jit(solution)/shard_map/finish/pallas_call | solution.py:626
Async XLA Ops:
  53.3 0.9 %copy-start = (f32[328,128]{1,0:T(8,128)S(1)}, f32[328,128]{1,0:T(8,128)}, u32[]{:S(2)}) copy-start(f32[328,128]{1,0:T(8,128)} %step.1.red) | copy-start | bytes 503812

commit v5 on v4

--- a/solution.py
+++ b/solution.py
@@ -87,8 +87,8 @@
 
 
 def step_kernel(
-    n, feat_in, row_in, col_in, target_in, k1_in, k2_in, ro, red,
-    feat, row_t, col_t, target, k1, k2,
+    n, feat_in, row_in, col_in, target_in, k1_in, k2_in, ro_in, red,
+    feat, row_t, col_t, target, k1, k2, ro,
     proj, sbuf, rbuf, tlow, thigh, roww, w1, wa, w2, rol, colr, mk, ts, act0, d0, act1, f1, d1, mis, g1,
     lhs, lhs2, k2t, res, qbuf, wq, xall, gall, fg, tacc, colacc, tiles, colp, rowg, cbuf, vbuf, arbuf, rsbuf, bbuf, mine, other, chip, gbuf,
     loads, sems,
@@ -110,7 +110,7 @@
     fetches = [
         pltpu.make_async_copy(source, place, loads.at[i])
         for i, (source, place) in enumerate(
-            ((feat_in, feat), (row_in, row_t), (col_in, col_t), (k1_in, k1), (k2_in, k2), (target_in, target))
+            ((feat_in, feat), (row_in, row_t), (col_in, col_t), (k1_in, k1), (k2_in, k2), (target_in, target), (ro_in, ro))
         )
     ]
     for fetch in fetches:
@@ -172,7 +172,7 @@
     for copy in gathers:
         copy.start()
 
-    for fetch in fetches[3:6]:
+    for fetch in fetches[3:7]:
         fetch.wait()
     rep8 = repeater(256)
     where_out = lax.shift_right_logical(iota((PAIR, 256), 1), 5)
@@ -528,7 +528,7 @@
     by_bin = dot(high[:, 0:64], weights) + dot(low[:, 0:64], weights)
     gbuf[256:288] = by_bin[:, 0:128]
     gbuf[288:320] = by_bin[:, 128:256]
-    keep = pltpu.make_async_copy(gbuf.at[pl.ds(256, 72)], red.at[pl.ds(256, 72)], loads.at[6])
+    keep = pltpu.make_async_copy(gbuf.at[pl.ds(256, 72)], red.at[pl.ds(256, 72)], loads.at[7])
     keep.start()
     all_of(rsbuf, sems.at[5])
     total = arbuf[chunk(plane), :]
@@ -551,7 +551,7 @@
     gbuf[chunk(plane), :] = total
     for s in range(1, side):
         send(gbuf.at[chunk(plane)], red.at[chunk(plane)], 8, across(s))
-    place = pltpu.make_async_copy(gbuf.at[chunk(plane)], red.at[chunk(plane)], loads.at[7])
+    place = pltpu.make_async_copy(gbuf.at[chunk(plane)], red.at[chunk(plane)], loads.at[8])
     place.start()
     all_of(bbuf.at[pl.ds(0, LINE - 1)], sems.at[6])
     all_of(rsbuf, sems.at[9])
@@ -598,7 +598,7 @@
     row_t, col_t = row_proj.T, col_proj.T
     hbm = pl.BlockSpec(memory_space=pltpu.HBM)
     scratch = dict(
-        feat=half(ROWS, 256), row_t=half(PAIR, 256), col_t=half(PAIR, 256), target=real(ROWS, 256), k1=half(288, PAIR), k2=half(288, PAIR),
+        feat=half(ROWS, 256), row_t=half(PAIR, 256), col_t=half(PAIR, 256), target=real(ROWS, 256), k1=half(288, PAIR), k2=half(288, PAIR), ro=half(1, PAIR),
         proj=real(32, 128), sbuf=real(16, 128), rbuf=real(AHEAD + 2, 16, 128), tlow=real(8, 256), thigh=real(8, 256),
         roww=real(24, 128), w1=half(1152, 256), wa=half(1152, 256), w2=real(72, 128), rol=real(8, 128),
         colr=real(LENGTH, 128), mk=pltpu.VMEM((LENGTH, 128), jnp.int32), ts=real(LENGTH, 128),
@@ -609,12 +609,12 @@
         xall=half(8 * WIDE, 768), gall=half(8 * WIDE, 256), fg=real(256, 768), tacc=real(80, 128),
         colacc=real(LENGTH, 128), tiles=real(288, 256), colp=real(72, 128), rowg=real(8, 128),
         cbuf=real(REACH, 8, 128), vbuf=real(2, 32, 128), arbuf=real(256, 128), rsbuf=real(side - 1, part, 128),
-        bbuf=real(LINE, part, 128), mine=real(part, 128), other=real(part, 128), chip=real(part, 128), gbuf=real(328, 128), loads=SEM((8,)), sems=SEM((12,)),
+        bbuf=real(LINE, part, 128), mine=real(part, 128), other=real(part, 128), chip=real(part, 128), gbuf=real(328, 128), loads=SEM((9,)), sems=SEM((12,)),
     )
     red = pl.pallas_call(
         functools.partial(step_kernel, n),
         out_shape=shape(328, 128),
-        in_specs=[hbm] * 6 + [vmem],
+        in_specs=[hbm] * 7,
         out_specs=hbm,
         scratch_shapes=list(scratch.values()),
         compiler_params=pltpu.CompilerParams(

time: 55.3 us -> 54.7 us (0.989)
  Pallas kernels: 53.6 us -> 53 us
    pallas_call x1, Pallas kernels: 52.7 us -> 52.1 us  [shards(): pl.pallas_call(functools.partial(step_kernel, n), out_shape=shape(328, 12...]
where the time goes in v5:
time: 54.7 us; the launch traced here: 54.5 us
  Pallas kernels  53 us (97%)
  local copies, waits for them, and re-layouts  0.91 us (2%)
  between operations  0.65 us (1%)
    pallas_call x1, Pallas kernels, shards(): pl.pallas_call(functools.partial(step_kernel, n), out_shape=shape(328, 12...  52.1 us

profile of v5, /device:TPU:1, one launch (start us, length us, event | category | flops | bytes accessed | tf_op | source)
XLA Modules:
  0.0 54.5 jit_solution(16382972669985323164)
XLA Ops:
  0.6 52.1 %step.1.red = f32[328,128]{1,0:T(8,128)} custom-call(bf16[32,256]{1,0:T(8,128)(2,1)} %feat_in.1, bf16[32,256]{1,0:T(8,128)(2,1)} %bitcast.12, bf16[32,256]{1,0:T(8,128)(2,1)} %bitcast.13, f32[32,256]{1,0:T(8,128)} %target_in.1, bf16[288,32]{1,0:T(8,128)(2,1)} %bitcast.10, bf16[288,32]{1,0:T(8,128)(2,1)} %bitcast.11, bf16[1,32]{1,0:T(2,128)(2,1)} %bitcast.14), custom_call_target="tpu_custom_call" | custom-call | tf_op jit(solution)/shard_map/step/pallas_call | solution.py:614
  52.7 0.0 copy-start
  52.7 0.9 %copy-done = f32[328,128]{1,0:T(8,128)S(1)} copy-done((f32[328,128]{1,0:T(8,128)S(1)}, f32[328,128]{1,0:T(8,128)}, u32[]{:S(2)}) %copy-start) | copy-done | bytes 167960
  53.6 0.9 %finish.1 = (f32[32,256]{1,0:T(8,128)}, f32[32,256]{1,0:T(8,128)}, f32[32,256]{1,0:T(8,128)}, f32[288,32]{1,0:T(8,128)}, f32[288,32]{1,0:T(8,128)}, /*index=5*/f32[1,32]{1,0:T(1,128)}) custom-call(f32[328,128]{1,0:T(8,128)S(1)} %copy-done), custom_call_target="tpu_custom_call" | custom-call | tf_op jit(solution)/shard_map/finish/pallas_call | solution.py:626
Async XLA Ops:
  52.7 0.9 %copy-start = (f32[328,128]{1,0:T(8,128)S(1)}, f32[328,128]{1,0:T(8,128)}, u32[]{:S(2)}) copy-start(f32[328,128]{1,0:T(8,128)} %step.1.red) | copy-start | bytes 503812

commit v6 on v5

--- a/solution.py
+++ b/solution.py
@@ -122,11 +122,11 @@
             pl.semaphore_signal(barrier, inc=1, device_id=(target_device,), device_id_type=MESH)
 
     def greet(sign, s, carry):
-        pl.semaphore_signal(barrier, inc=1, device_id=(me + sign * s,), device_id_type=MESH)
+        pl.semaphore_signal(barrier, inc=1, device_id=(me + sign * 2 * s,), device_id_type=MESH)
         return carry
 
-    lax.fori_loop(AHEAD + 1, SIDE - pos, functools.partial(greet, 1), 0)
-    lax.fori_loop(AHEAD + 1, pos + 1, functools.partial(greet, -1), 0)
+    lax.fori_loop(AHEAD // 2 + 1, LINE - depth, functools.partial(greet, 1), 0)
+    lax.fori_loop(AHEAD // 2 + 1, depth + 1, functools.partial(greet, -1), 0)
 
     def greet_across(s, carry):
         pl.semaphore_signal(barrier, inc=1, device_id=(across(s),), device_id_type=MESH)
@@ -146,7 +146,7 @@
         col_c = jnp.where(where_block == b, cc[8 * b : 8 * b + 8], col_c)
     sbuf[0:8] = col_c
     sbuf[8:16] = row_c
-    greeted = jnp.maximum(SIDE - AHEAD - 1 - pos, 0) + jnp.maximum(pos - AHEAD, 0)
+    greeted = jnp.maximum(LINE - AHEAD // 2 - 1 - depth, 0) + jnp.maximum(depth - AHEAD // 2, 0)
     pl.semaphore_wait(barrier, 2 * AHEAD + greeted + side - 1)
     gathers = []
     for m in range(AHEAD + 1, 2, -1):
@@ -536,14 +536,12 @@
         total = total + rsbuf[s - 1]
     mine[...] = total
     send(mine, other, 10, me + 1 - 2 * lax.rem(me, 2))
-    all_of(rsbuf, sems.at[4])
     all_of(other, sems.at[11])
     total = total + other[...]
     chip[...] = total
     bbuf[depth] = total
     for s in range(1, LINE):
         send(chip, bbuf.at[depth], 6, me + 2 * (lax.rem(depth + s, LINE) - depth))
-    all_of(other, sems.at[10])
     all_of(bbuf.at[pl.ds(0, LINE - 1)], sems.at[7])
     total = bbuf[0]
     for q in range(1, LINE):
@@ -556,6 +554,8 @@
     all_of(bbuf.at[pl.ds(0, LINE - 1)], sems.at[6])
     all_of(rsbuf, sems.at[9])
     all_of(rsbuf, sems.at[8])
+    all_of(rsbuf, sems.at[4])
+    all_of(other, sems.at[10])
     keep.wait()
     place.wait()
 

time: 54.7 us -> 54.5 us (level)
  no operation moved by 1% of the time
where the time goes in v6:
time: 54.5 us; the launch traced here: 54.3 us
  Pallas kernels  52.8 us (97%)
  local copies, waits for them, and re-layouts  0.91 us (2%)
  between operations  0.65 us (1%)
    pallas_call x1, Pallas kernels, shards(): pl.pallas_call(functools.partial(step_kernel, n), out_shape=shape(328, 12...  51.9 us

profile of v6, /device:TPU:1, one launch (start us, length us, event | category | flops | bytes accessed | tf_op | source)
XLA Modules:
  0.0 54.3 jit_solution(17983941159750638974)
XLA Ops:
  0.6 51.9 %step.1.red = f32[328,128]{1,0:T(8,128)} custom-call(bf16[32,256]{1,0:T(8,128)(2,1)} %feat_in.1, bf16[32,256]{1,0:T(8,128)(2,1)} %bitcast.12, bf16[32,256]{1,0:T(8,128)(2,1)} %bitcast.13, f32[32,256]{1,0:T(8,128)} %target_in.1, bf16[288,32]{1,0:T(8,128)(2,1)} %bitcast.10, bf16[288,32]{1,0:T(8,128)(2,1)} %bitcast.11, bf16[1,32]{1,0:T(2,128)(2,1)} %bitcast.14), custom_call_target="tpu_custom_call" | custom-call | tf_op jit(solution)/shard_map/step/pallas_call | solution.py:614
  52.5 0.0 copy-start
  52.5 0.9 %copy-done = f32[328,128]{1,0:T(8,128)S(1)} copy-done((f32[328,128]{1,0:T(8,128)S(1)}, f32[328,128]{1,0:T(8,128)}, u32[]{:S(2)}) %copy-start) | copy-done | bytes 167960
  53.4 0.9 %finish.1 = (f32[32,256]{1,0:T(8,128)}, f32[32,256]{1,0:T(8,128)}, f32[32,256]{1,0:T(8,128)}, f32[288,32]{1,0:T(8,128)}, f32[288,32]{1,0:T(8,128)}, /*index=5*/f32[1,32]{1,0:T(1,128)}) custom-call(f32[328,128]{1,0:T(8,128)S(1)} %copy-done), custom_call_target="tpu_custom_call" | custom-call | tf_op jit(solution)/shard_map/finish/pallas_call | solution.py:626
Async XLA Ops:
  52.5 0.9 %copy-start = (f32[328,128]{1,0:T(8,128)S(1)}, f32[328,128]{1,0:T(8,128)}, u32[]{:S(2)}) copy-start(f32[328,128]{1,0:T(8,128)} %step.1.red) | copy-start | bytes 503812
